TPU v7x, 128 devices: a whole 4x4x4 slice. The times are simulated.
128 devices in a mesh: dp: 32 (over z, x, core), col: 4 (over y).
Axes of the slice: x: 4, y: 4, z: 4, core: 2. Of those that a mesh axis runs over, the one named last changes fastest.
Arguments:
- activations: bfloat16 [16384, 16384], P('dp', 'col'), may hold values from -18 to 18
- out_grads: bfloat16 [16384, 53248], P('dp', 'col'), may hold values from -18 to 18
- sketch: bfloat16 [53248, 128], P('col'), may hold values from -6 to 6
Outputs:
- adapter_b: float32 [16384, 64], P(('col', 'dp'))
- adapter_a_t: float32 [53248, 64], P(('col', 'dp'))
All inputs are finite; a program needn't handle non-finite values.
Results may differ from a plain program's by a relative error of at most 0.005.
Values may be sent and summed in bfloat16 or wider, within the bound.
A program may use at most 128 MiB of HBM per device.

v0:
```python
import jax
import jax.numpy as jnp
from jax import lax
from jax.sharding import PartitionSpec as P

D = 16384
F = 53248
RANK = 64
ITERS = 2


def copy_for_each(x, axis):
    count = lax.axis_size(axis)
    return lax.all_to_all(jnp.broadcast_to(x[None], (count, *x.shape)), axis, 0, 0, tiled=True)


def over_copies(x, axis):
    everything = copy_for_each(x, axis)
    return jnp.sum(everything, axis=0)


def cut_along(x, dim, count):
    lengths = x.shape
    pieces = x.reshape(*lengths[:dim], count, lengths[dim] // count, *lengths[dim + 1 :])
    return jnp.moveaxis(pieces, dim, 0)


def sum_at_owner(x, axis, dim):
    count = lax.axis_size(axis)
    pieces = lax.all_to_all(cut_along(x, dim, count), axis, 0, 0, tiled=True)
    return jnp.sum(pieces, axis=0)


def total_of_pieces(x, axis):
    return lax.all_gather(x, axis).sum(0)


def laid_out(pieces, dim):
    pieces = jnp.moveaxis(pieces, 0, dim)
    lengths = pieces.shape
    return pieces.reshape(*lengths[:dim], lengths[dim] * lengths[dim + 1], *lengths[dim + 2 :])


def gather_directly(x, axis, dim):
    pieces = copy_for_each(x, axis)
    return laid_out(pieces, dim)


def cholesky_basis(panel_in, gram_matrix, row_total):
    width = panel_in.shape[1]
    identity_k = jnp.eye(width, dtype=jnp.float32)
    shift_value = 1e-05 * jnp.trace(gram_matrix) / width
    lower_factor = jnp.linalg.cholesky(gram_matrix + shift_value * identity_k)
    inverse = jax.scipy.linalg.solve_triangular(lower_factor, identity_k, lower=True)
    scaled = jnp.dot(
        panel_in, inverse.T, precision=lax.Precision.HIGHEST, preferred_element_type=jnp.float32
    )
    return scaled * jnp.float32(row_total**0.5)


def local_gram(panel_in):
    return jnp.dot(
        panel_in.T, panel_in, precision=lax.Precision.HIGHEST, preferred_element_type=jnp.float32
    )


def body(activations, out_grads, sketch):
    dp_count = lax.axis_size("dp")
    hidden_local = out_grads.shape[1]
    hidden_rows = hidden_local // dp_count
    right_b = sketch
    left_rows_q = None
    right_rows_p = None
    for iteration in range(ITERS):
        left_part = jnp.dot(out_grads, right_b, preferred_element_type=jnp.float32)
        left_s = over_copies(left_part, "col").astype(jnp.bfloat16)
        left_y = sum_at_owner(
            lax.dot_general(
                activations, left_s, (((0,), (0,)), ((), ())), preferred_element_type=jnp.float32
            ),
            "dp",
            0,
        )
        gram_left = total_of_pieces(local_gram(left_y), ("dp", "col"))
        left_rows_q = cholesky_basis(left_y, gram_left, D)
        left_b = left_rows_q.astype(jnp.bfloat16)
        right_part = jnp.dot(
            activations, gather_directly(left_b, "dp", 0), preferred_element_type=jnp.float32
        )
        right_t = over_copies(right_part, "col").astype(jnp.bfloat16)
        whole_part = lax.dot_general(
            out_grads, right_t, (((0,), (0,)), ((), ())), preferred_element_type=jnp.float32
        )
        right_full = lax.psum(whole_part, "dp")
        gram_right = over_copies(local_gram(right_full), "col")
        right_whole_p = cholesky_basis(right_full, gram_right, F)
        right_b = right_whole_p.astype(jnp.bfloat16)
        right_rows_p = lax.dynamic_slice_in_dim(
            right_whole_p, lax.axis_index("dp") * hidden_rows, hidden_rows, 0
        )
    return (left_rows_q[:, :RANK], right_rows_p[:, RANK:])


def solution(mesh):
    return jax.shard_map(
        body,
        mesh=mesh,
        in_specs=(P("dp", "col"), P("dp", "col"), P("col", None)),
        out_specs=(P(("col", "dp"), None), P(("col", "dp"), None)),
        check_vma=False,
    )
```

profile of v0, /device:TPU:6, one launch (start us, length us, event | category | flops | bytes accessed | tf_op | source)
XLA Modules:
  0.0 803.6 jit_solution(13290955720750246626)
XLA Ops:
  7.2 1.9 copy-done
  9.1 7.1 fusion.27
  16.3 19.4 %all_to_all.50 = f32[4,512,128]{2,1,0:T(8,128)S(1)} all-to-all(f32[4,512,128]{2,1,0:T(8,128)S(1)} %broadcast_in_dim.24), channel_id=1, replica_groups=mesh['dp'=32,'col'=4] {'col'}, dimensions={0} | all-to-all | bytes 2097152 | tf_op jit(solution)/shard_map/all_to_all | solution.py:14
  35.7 2.9 convolution_bitcast_fusion.3
  38.6 0.2 copy.63
  38.9 34.1 %all_to_all.51 = f32[32,128,128]{1,2,0:T(8,128)S(1)} all-to-all(f32[32,128,128]{1,2,0:T(8,128)S(1)} %bitcast.97), channel_id=1, replica_groups=mesh['dp'=32,'col'=4] {'dp'}, dimensions={0} | all-to-all | bytes 4194304 | tf_op jit(solution)/shard_map/all_to_all | solution.py:30
  73.1 0.9 fusion.28
  74.0 66.9 %all-gather.5.cloned.1.call-done = f32[16384,128]{1,0:T(8,128)} async-done(((f32[128,128]{1,0:T(8,128)}), f32[16384,128]{1,0:T(8,128)}) %all-gather.5.cloned.1.call-update) | async-done | bytes 8388624 | tf_op jit(solution)/shard_map/all_gather | solution.py:35
  140.9 3.8 reduce_sum.120
  144.8 0.6 select_reduce_fusion.7
  146.3 11.7 %cholesky.74 = f32[128,128]{1,0:T(8,128)S(1)} custom-call(f32[128,128]{1,0:T(8,128)S(1)} %fusion.25), custom_call_target="Cholesky" | custom-call | tf_op jit(solution)/shard_map/jit(cholesky)/cholesky | solution.py:53
  158.0 0.6 compare_reduce_fusion.3
  158.6 0.7 fusion.14
  159.3 9.8 %custom-call.8 = f32[1,128,128]{1,2,0:T(8,128)S(1)} custom-call(f32[1,128,128]{2,1,0:T(8,128)S(1)} %fusion.14), custom_call_target="InvertDiagBlocksLowerTriangular" | custom-call | tf_op jit(solution)/shard_map/jit(_solve_triangular)/triangular_solve | solution.py:54
  169.1 0.3 fusion.8
  169.4 0.3 fusion.1
  169.9 21.4 %all_to_all.52 = bf16[32,128,128]{2,1,0:T(8,128)(2,1)S(1)} all-to-all(bf16[32,128,128]{2,1,0:T(8,128)(2,1)S(1)} %broadcast_in_dim.26), channel_id=1, replica_groups=mesh['dp'=32,'col'=4] {'dp'}, dimensions={0} | all-to-all | bytes 2097152 | tf_op jit(solution)/shard_map/all_to_all | solution.py:14
  191.3 3.7 convolution_bitcast_fusion.5
  195.2 19.4 %all_to_all.53 = f32[4,512,128]{2,1,0:T(8,128)S(1)} all-to-all(f32[4,512,128]{2,1,0:T(8,128)S(1)} %broadcast_in_dim.27), channel_id=1, replica_groups=mesh['dp'=32,'col'=4] {'col'}, dimensions={0} | all-to-all | bytes 2097152 | tf_op jit(solution)/shard_map/all_to_all | solution.py:14
  214.6 9.8 %convolution_bitcast_fusion.1 = f32[13312,128]{0,1:T(8,128)} fusion(bf16[512,13312]{1,0:T(8,128)(2,1)} %param.7, bf16[512,128]{1,0:T(8,128)(2,1)S(1)} %reduce_sum.122), kind=kOutput, calls=%fused_computation.2 | convolution fusion | flops 1744830464 | bytes 20578304 | tf_op jit(solution)/shard_map/dot_general | solution.py:91
  224.5 114.8 %all-reduce.3.cloned.1.call-done = f32[13312,128]{0,1:T(8,128)} async-done(((f32[13312,128]{0,1:T(8,128)}), f32[13312,128]{0,1:T(8,128)}) %all-reduce.3.cloned.1.call-update) | async-done | bytes 6815760 | tf_op jit(solution)/shard_map/psum | solution.py:94
  339.3 8.8 %fusion.29 = f32[128,128]{1,0:T(8,128)S(1)} fusion(f32[13312,128]{0,1:T(8,128)} %all-reduce.3.cloned.1.call-done), kind=kOutput, calls=%fused_computation.69 | convolution fusion | flops 2617245696 | bytes 6881280 | tf_op jit(solution)/shard_map/dot_general | solution.py:62
  348.1 10.8 %all_to_all.54 = f32[4,128,128]{2,1,0:T(8,128)S(1)} all-to-all(f32[4,128,128]{2,1,0:T(8,128)S(1)} %broadcast_in_dim.28), channel_id=1, replica_groups=mesh['dp'=32,'col'=4] {'col'}, dimensions={0} | all-to-all | bytes 524288 | tf_op jit(solution)/shard_map/all_to_all | solution.py:14
  359.0 0.6 select_reduce_fusion.6
  360.4 11.7 %cholesky.85 = f32[128,128]{1,0:T(8,128)S(1)} custom-call(f32[128,128]{1,0:T(8,128)S(1)} %fusion.23), custom_call_target="Cholesky" | custom-call | tf_op jit(solution)/shard_map/jit(cholesky)/cholesky | solution.py:53
  372.1 0.6 compare_reduce_fusion.2
  372.8 0.7 fusion.15
  373.4 9.8 %custom-call.9 = f32[1,128,128]{1,2,0:T(8,128)S(1)} custom-call(f32[1,128,128]{2,1,0:T(8,128)S(1)} %fusion.15), custom_call_target="InvertDiagBlocksLowerTriangular" | custom-call | tf_op jit(solution)/shard_map/jit(_solve_triangular)/triangular_solve | solution.py:54
  383.3 0.3 fusion.6
  383.5 22.8 %fusion = bf16[13312,128]{1,0:T(8,128)(2,1)S(1)} fusion(f32[13312,128]{0,1:T(8,128)} %all-reduce.3.cloned.1.call-done, f32[128,128]{1,0:T(8,128)S(1)} %fusion.6), kind=kOutput, calls=%fused_computation.3 | convolution fusion | flops 2620653568 | bytes 10289152 | tf_op jit(solution)/shard_map/dot_general | solution.py:55
  406.3 10.2 %convolution_bitcast_fusion.6 = f32[512,128]{0,1:T(8,128)} fusion(bf16[13312,128]{1,0:T(8,128)(2,1)S(1)} %fusion, bf16[512,13312]{1,0:T(8,128)(2,1)} %param.7), kind=kOutput, calls=%fused_computation.10 | convolution fusion | flops 1744830464 | bytes 17301504 | tf_op jit(solution)/shard_map/dot_general | solution.py:75
  416.5 1.1 copy.42
  417.7 14.9 %all_to_all.55 = f32[4,512,128]{2,1,0:T(8,128)S(1)} all-to-all(f32[4,512,128]{2,1,0:T(8,128)S(1)} %broadcast_in_dim.29), channel_id=1, replica_groups=mesh['dp'=32,'col'=4] {'col'}, dimensions={0} | all-to-all | bytes 2097152 | tf_op jit(solution)/shard_map/all_to_all | solution.py:14
  432.6 2.9 convolution_bitcast_fusion.2
  435.8 33.7 %all_to_all.56 = f32[32,128,128]{1,2,0:T(8,128)S(1)} all-to-all(f32[32,128,128]{1,2,0:T(8,128)S(1)} %bitcast.98), channel_id=1, replica_groups=mesh['dp'=32,'col'=4] {'dp'}, dimensions={0} | all-to-all | bytes 4194304 | tf_op jit(solution)/shard_map/all_to_all | solution.py:30
  469.6 0.9 fusion.30
  470.6 66.9 %all-gather.7.cloned.1.call-done = f32[16384,128]{1,0:T(8,128)} async-done(((f32[128,128]{1,0:T(8,128)}), f32[16384,128]{1,0:T(8,128)}) %all-gather.7.cloned.1.call-update) | async-done | bytes 8388624 | tf_op jit(solution)/shard_map/all_gather | solution.py:35
  537.5 3.8 reduce_sum.127
  541.4 0.6 select_reduce_fusion.5
  542.8 11.7 %cholesky.96 = f32[128,128]{1,0:T(8,128)S(1)} custom-call(f32[128,128]{1,0:T(8,128)S(1)} %fusion.21), custom_call_target="Cholesky" | custom-call | tf_op jit(solution)/shard_map/jit(cholesky)/cholesky | solution.py:53
  554.6 0.6 compare_reduce_fusion.1
  555.2 0.7 fusion.16
  555.9 9.8 %custom-call.10 = f32[1,128,128]{1,2,0:T(8,128)S(1)} custom-call(f32[1,128,128]{2,1,0:T(8,128)S(1)} %fusion.16), custom_call_target="InvertDiagBlocksLowerTriangular" | custom-call | tf_op jit(solution)/shard_map/jit(_solve_triangular)/triangular_solve | solution.py:54
  565.7 0.3 fusion.4
  566.0 0.3 fusion.26
  566.5 21.0 %all_to_all.57 = bf16[32,128,128]{2,1,0:T(8,128)(2,1)S(1)} all-to-all(bf16[32,128,128]{2,1,0:T(8,128)(2,1)S(1)} %broadcast_in_dim.30), channel_id=1, replica_groups=mesh['dp'=32,'col'=4] {'dp'}, dimensions={0} | all-to-all | bytes 2097152 | tf_op jit(solution)/shard_map/all_to_all | solution.py:14
  587.5 3.7 convolution_bitcast_fusion.4
  591.4 19.5 %all_to_all.58 = f32[4,512,128]{2,1,0:T(8,128)S(1)} all-to-all(f32[4,512,128]{2,1,0:T(8,128)S(1)} %broadcast_in_dim.31), channel_id=1, replica_groups=mesh['dp'=32,'col'=4] {'col'}, dimensions={0} | all-to-all | bytes 2097152 | tf_op jit(solution)/shard_map/all_to_all | solution.py:14
  610.9 9.8 %convolution_bitcast_fusion = f32[13312,128]{0,1:T(8,128)} fusion(bf16[512,13312]{1,0:T(8,128)(2,1)} %param.7, bf16[512,128]{1,0:T(8,128)(2,1)S(1)} %reduce_sum.129), kind=kOutput, calls=%fused_computation | convolution fusion | flops 1744830464 | bytes 20578304 | tf_op jit(solution)/shard_map/dot_general | solution.py:91
  620.7 115.3 %all-reduce.5.cloned.1.call-done = f32[13312,128]{0,1:T(8,128)} async-done(((f32[13312,128]{0,1:T(8,128)}), f32[13312,128]{0,1:T(8,128)}) %all-reduce.5.cloned.1.call-update) | async-done | bytes 6815760 | tf_op jit(solution)/shard_map/psum | solution.py:94
  736.0 8.8 %fusion.31 = f32[128,128]{1,0:T(8,128)S(1)} fusion(f32[13312,128]{0,1:T(8,128)} %all-reduce.5.cloned.1.call-done), kind=kOutput, calls=%fused_computation.71 | convolution fusion | flops 2617245696 | bytes 6881280 | tf_op jit(solution)/shard_map/dot_general | solution.py:62
  744.7 0.7 broadcast_in_dim.32
  745.5 4.3 all-to-all-start.9
  749.7 0.7 copy.53
  750.4 6.0 all-to-all-done.9
  756.5 0.6 select_reduce_fusion.4
  758.0 11.7 %cholesky.107 = f32[128,128]{1,0:T(8,128)S(1)} custom-call(f32[128,128]{1,0:T(8,128)S(1)} %fusion.19), custom_call_target="Cholesky" | custom-call | tf_op jit(solution)/shard_map/jit(cholesky)/cholesky | solution.py:53
  769.7 0.6 compare_reduce_fusion
  770.4 0.7 fusion.17
  771.0 9.8 %custom-call.11 = f32[1,128,128]{1,2,0:T(8,128)S(1)} custom-call(f32[1,128,128]{2,1,0:T(8,128)S(1)} %fusion.17), custom_call_target="InvertDiagBlocksLowerTriangular" | custom-call | tf_op jit(solution)/shard_map/jit(_solve_triangular)/triangular_solve | solution.py:54
  780.8 0.3 fusion.2
  781.1 13.1 %fusion.32 = f32[13312,128]{1,0:T(8,128)S(1)} fusion(f32[13312,128]{0,1:T(8,128)} %all-reduce.5.cloned.1.call-done, f32[128,128]{1,0:T(8,128)S(1)} %fusion.2), kind=kOutput, calls=%fused_computation.72 | convolution fusion | flops 2617245696 | bytes 13697024 | tf_op jit(solution)/shard_map/dot_general | solution.py:55
  794.2 0.8 dynamic-slice_multiply_fusion
  795.0 1.7 copy.54
  (49 shorter events, 2.9 us)
Async XLA Ops:
  7.2 2.0 copy-start
  7.2 133.8 %all-gather.5.cloned.1.call-start = ((), (), s32[]{:S(2)}) async-start(), calls=%async_computation.12 | async-start | bytes 8454144 | tf_op jit(solution)/shard_map/all_gather | solution.py:35
  74.0 265.3 %all-reduce.3.cloned.1.call-start = ((), (), s32[]{:S(2)}) async-start(), calls=%async_computation.10 | async-start | bytes 13631488 | tf_op jit(solution)/shard_map/psum | solution.py:94
  224.4 313.1 %all-gather.7.cloned.1.call-start = ((), (), s32[]{:S(2)}) async-start(), calls=%async_computation.13 | async-start | bytes 8454144 | tf_op jit(solution)/shard_map/all_gather | solution.py:35
  470.6 265.4 %all-reduce.5.cloned.1.call-start = ((), (), s32[]{:S(2)}) async-start(), calls=%async_computation.11 | async-start | bytes 13631488 | tf_op jit(solution)/shard_map/psum | solution.py:94
  745.5 11.0 %all-to-all-start.9 = ((f32[4,128,128]{2,1,0:T(8,128)}), f32[4,128,128]{2,1,0:T(8,128)S(1)}, u32[]{:S(2)}, u32[]{:S(2)}) async-start(f32[4,128,128]{2,1,0:T(8,128)} %broadcast_in_dim.32), calls=%async_computation.9 | async-start | bytes 524288 | tf_op jit(solution)/shard_map/all_to_all | solution.py:14
  780.8 15.9 %copy-start.1 = (bf16[13312,128]{1,0:T(8,128)(2,1)S(1)}, bf16[13312,128]{1,0:T(8,128)(2,1)}, u32[]{:S(2)}) copy-start(bf16[13312,128]{1,0:T(8,128)(2,1)} %param.8) | copy-start | bytes 10223620
Sparse Core Ops, SparseCore 0:
  74.1 66.7 all-gather.4
  224.6 114.6 all-reduce.2
  470.7 66.7 all-gather.6
  620.8 115.1 all-reduce.4
where the time goes:
time: 813 us; the launch traced here: 804 us
  waiting for transfers between devices  370 us (46%)
  blocking collectives  194 us (24%)
  matrix products  107 us (13%)
  other arithmetic  103 us (13%)
  between operations  17.2 us (2%)
  local copies, waits for them, and re-layouts  8.32 us (1%)
    psum x2, waiting for transfers between devices, body(): right_full = lax.psum(whole_part, 'dp')  230 us
    all_gather x2, waiting for transfers between devices, total_of_pieces(): return lax.all_gather(x, axis).sum(0)  134 us
    all_to_all x7, blocking collectives, copy_for_each(): lax.all_to_all(jnp.broadcast_to(x[None], (count, *x.shape)), axis, 0, 0,...  126 us
    all_to_all x2, blocking collectives, sum_at_owner(): pieces = lax.all_to_all(cut_along(x, dim, count), axis, 0, 0, tiled=True)  67.8 us
    another operation x12, other arithmetic, cholesky_basis(): lower_factor = jnp.linalg.cholesky(gram_matrix + shift_value * identity_k)  49.6 us
    another operation x8, other arithmetic, cholesky_basis(): jax.scipy.linalg.solve_triangular(lower_factor, identity_k, lower=True)  41.9 us
    dot_general x4, matrix products, cholesky_basis(): jnp.dot(panel_in, inverse.T, precision=lax.Precision.HIGHEST, preferred_e...  36.4 us
    dot_general x2, matrix products, body(): lax.dot_general(out_grads, right_t, (((0,), (0,)), ((), ())), preferred_e...  19.5 us
  transfers between devices with their start and end apart: 5, of which 5 were waited for; matrix products, arithmetic and copies ran while one was open for 0% of the time, Pallas kernels for 0%

commit v1 on v0

--- a/solution.py
+++ b/solution.py
@@ -91,7 +91,11 @@
         whole_part = lax.dot_general(
             out_grads, right_t, (((0,), (0,)), ((), ())), preferred_element_type=jnp.float32
         )
-        right_full = lax.psum(whole_part, "dp")
+        right_full = whole_part
+        for hop in (1, 2, 4, 8, 16):
+            right_full = right_full + lax.ppermute(
+                right_full, "dp", [(dev, dev ^ hop) for dev in range(32)]
+            )
         gram_right = over_copies(local_gram(right_full), "col")
         right_whole_p = cholesky_basis(right_full, gram_right, F)
         right_b = right_whole_p.astype(jnp.bfloat16)

time: 813 us -> 1830 us (2.25)
  waiting for transfers between devices: 370 us -> 1340 us
  other arithmetic: 103 us -> 164 us
  matrix products: 107 us -> 85.1 us
    ppermute x0 -> x10, waiting for transfers between devices: none -> 1200 us  [body(): lax.ppermute(right_full, 'dp', [(dev, dev ^ hop) for dev in range(32)])]
    psum x2 -> x0, waiting for transfers between devices: 230 us -> none  [body(): right_full = lax.psum(whole_part, 'dp')]
    add x0 -> x10, other arithmetic: none -> 61.2 us  [body(): right_full + lax.ppermute(right_full, 'dp', [(dev, dev ^ hop) for dev in...]
  transfers between devices with their start and end apart: 5 -> 13, of which waited for: 5 -> 13; matrix products, arithmetic and copies ran while one was open for 0% -> 0% of each run, Pallas kernels for 0% -> 0%
where the time goes in v1:
time: 1830 us; the launch traced here: 1820 us
  waiting for transfers between devices  1340 us (73%)
  blocking collectives  189 us (10%)
  other arithmetic  164 us (9%)
  matrix products  85.1 us (5%)
    ppermute x10, waiting for transfers between devices, body(): lax.ppermute(right_full, 'dp', [(dev, dev ^ hop) for dev in range(32)])  1200 us
    all_gather x2, waiting for transfers between devices, total_of_pieces(): return lax.all_gather(x, axis).sum(0)  134 us
    all_to_all x7, blocking collectives, copy_for_each(): lax.all_to_all(jnp.broadcast_to(x[None], (count, *x.shape)), axis, 0, 0,...  123 us
    all_to_all x2, blocking collectives, sum_at_owner(): pieces = lax.all_to_all(cut_along(x, dim, count), axis, 0, 0, tiled=True)  66.4 us
    add x10, other arithmetic, body(): right_full + lax.ppermute(right_full, 'dp', [(dev, dev ^ hop) for dev in...  61.2 us
    another operation x12, other arithmetic, cholesky_basis(): lower_factor = jnp.linalg.cholesky(gram_matrix + shift_value * identity_k)  49.6 us
    another operation x8, other arithmetic, cholesky_basis(): jax.scipy.linalg.solve_triangular(lower_factor, identity_k, lower=True)  41.9 us
  transfers between devices with their start and end apart: 13, of which 13 were waited for; matrix products, arithmetic and copies ran while one was open for 0% of the time, Pallas kernels for 0%

profile of v1, /device:TPU:6, one launch (start us, length us, event | category | flops | bytes accessed | tf_op | source)
XLA Modules:
  0.0 1818.3 jit_solution(11841801174601405542)
XLA Ops:
  7.2 1.9 copy-done
  9.1 7.1 fusion.27
  16.3 19.4 %all_to_all.50 = f32[4,512,128]{2,1,0:T(8,128)S(1)} all-to-all(f32[4,512,128]{2,1,0:T(8,128)S(1)} %broadcast_in_dim.24), channel_id=1, replica_groups=mesh['dp'=32,'col'=4] {'col'}, dimensions={0} | all-to-all | bytes 2097152 | tf_op jit(solution)/shard_map/all_to_all | solution.py:14
  35.7 2.9 convolution_bitcast_fusion.3
  38.9 34.1 %all_to_all.51 = f32[32,128,128]{1,2,0:T(8,128)S(1)} all-to-all(f32[32,128,128]{1,2,0:T(8,128)S(1)} %bitcast.97), channel_id=1, replica_groups=mesh['dp'=32,'col'=4] {'dp'}, dimensions={0} | all-to-all | bytes 4194304 | tf_op jit(solution)/shard_map/all_to_all | solution.py:30
  74.0 66.9 %all-gather.5.cloned.1.call-done = f32[16384,128]{1,0:T(8,128)} async-done(((f32[128,128]{1,0:T(8,128)}), f32[16384,128]{1,0:T(8,128)}) %all-gather.5.cloned.1.call-update) | async-done | bytes 8388624 | tf_op jit(solution)/shard_map/all_gather | solution.py:35
  140.9 3.8 reduce_sum.120
  146.3 11.7 cholesky.74
  159.3 9.8 custom-call.8
  169.9 21.3 %all_to_all.52 = bf16[32,128,128]{2,1,0:T(8,128)(2,1)S(1)} all-to-all(bf16[32,128,128]{2,1,0:T(8,128)(2,1)S(1)} %broadcast_in_dim.26), channel_id=1, replica_groups=mesh['dp'=32,'col'=4] {'dp'}, dimensions={0} | all-to-all | bytes 2097152 | tf_op jit(solution)/shard_map/all_to_all | solution.py:14
  191.2 3.7 convolution_bitcast_fusion.5
  195.1 19.4 %all_to_all.53 = f32[4,512,128]{2,1,0:T(8,128)S(1)} all-to-all(f32[4,512,128]{2,1,0:T(8,128)S(1)} %broadcast_in_dim.27), channel_id=1, replica_groups=mesh['dp'=32,'col'=4] {'col'}, dimensions={0} | all-to-all | bytes 2097152 | tf_op jit(solution)/shard_map/all_to_all | solution.py:14
  214.6 7.0 convolution_bitcast_fusion.1
  221.8 2.6 copy-done.4
  224.4 8.3 collective-permute-done
  232.7 5.7 add.55
  238.7 148.7 %collective-permute-done.1 = f32[13312,128]{0,1:T(8,128)} collective-permute-done((f32[13312,128]{0,1:T(8,128)S(1)}, f32[13312,128]{0,1:T(8,128)}, u32[]{:S(2)}, u32[]{:S(2)}) %collective-permute-start.1) | collective-permute-done | bytes 6815776 | tf_op jit(solution)/shard_map/ppermute | solution.py:96
  387.4 6.7 add.56
  394.1 1.7 collective-permute-start.2
  395.9 148.0 %collective-permute-done.2 = f32[13312,128]{0,1:T(8,128)} collective-permute-done((f32[13312,128]{0,1:T(8,128)}, f32[13312,128]{0,1:T(8,128)}, u32[]{:S(2)}, u32[]{:S(2)}) %collective-permute-start.2) | collective-permute-done | bytes 6815776 | tf_op jit(solution)/shard_map/ppermute | solution.py:96
  543.9 5.7 add.57
  550.3 146.5 %collective-permute-done.3 = f32[13312,128]{0,1:T(8,128)} collective-permute-done((f32[13312,128]{0,1:T(8,128)S(1)}, f32[13312,128]{0,1:T(8,128)}, u32[]{:S(2)}, u32[]{:S(2)}) %collective-permute-start.3) | collective-permute-done | bytes 6815776 | tf_op jit(solution)/shard_map/ppermute | solution.py:96
  696.9 6.7 add.58
  704.5 147.1 %collective-permute-done.4 = f32[13312,128]{0,1:T(8,128)} collective-permute-done((f32[13312,128]{0,1:T(8,128)}, f32[13312,128]{0,1:T(8,128)}, u32[]{:S(2)}, u32[]{:S(2)}) %collective-permute-start.4) | collective-permute-done | bytes 6815776 | tf_op jit(solution)/shard_map/ppermute | solution.py:96
  851.5 5.7 add.59
  857.3 5.4 fusion.29
  862.7 9.5 all_to_all.54
  873.7 11.7 cholesky.85
  886.8 9.8 custom-call.9
  896.9 13.1 fusion
  910.0 10.2 convolution_bitcast_fusion.6
  920.2 1.1 copy.42
  921.4 13.4 all_to_all.55
  934.8 2.9 convolution_bitcast_fusion.2
  938.0 32.3 %all_to_all.56 = f32[32,128,128]{1,2,0:T(8,128)S(1)} all-to-all(f32[32,128,128]{1,2,0:T(8,128)S(1)} %bitcast.98), channel_id=1, replica_groups=mesh['dp'=32,'col'=4] {'dp'}, dimensions={0} | all-to-all | bytes 4194304 | tf_op jit(solution)/shard_map/all_to_all | solution.py:30
  971.3 66.9 %all-gather.7.cloned.1.call-done = f32[16384,128]{1,0:T(8,128)} async-done(((f32[128,128]{1,0:T(8,128)}), f32[16384,128]{1,0:T(8,128)}) %all-gather.7.cloned.1.call-update) | async-done | bytes 8388624 | tf_op jit(solution)/shard_map/all_gather | solution.py:35
  1038.2 3.8 reduce_sum.127
  1043.6 11.7 cholesky.96
  1056.6 9.8 custom-call.10
  1067.3 21.0 %all_to_all.57 = bf16[32,128,128]{2,1,0:T(8,128)(2,1)S(1)} all-to-all(bf16[32,128,128]{2,1,0:T(8,128)(2,1)S(1)} %broadcast_in_dim.30), channel_id=1, replica_groups=mesh['dp'=32,'col'=4] {'dp'}, dimensions={0} | all-to-all | bytes 2097152 | tf_op jit(solution)/shard_map/all_to_all | solution.py:14
  1088.2 3.7 convolution_bitcast_fusion.4
  1092.1 19.2 %all_to_all.58 = f32[4,512,128]{2,1,0:T(8,128)S(1)} all-to-all(f32[4,512,128]{2,1,0:T(8,128)S(1)} %broadcast_in_dim.31), channel_id=1, replica_groups=mesh['dp'=32,'col'=4] {'col'}, dimensions={0} | all-to-all | bytes 2097152 | tf_op jit(solution)/shard_map/all_to_all | solution.py:14
  1111.4 7.0 convolution_bitcast_fusion
  1119.1 2.2 copy-done.5
  1121.2 8.7 collective-permute-done.5
  1130.0 5.7 add.62
  1136.3 148.4 %collective-permute-done.6 = f32[13312,128]{0,1:T(8,128)} collective-permute-done((f32[13312,128]{0,1:T(8,128)S(1)}, f32[13312,128]{0,1:T(8,128)}, u32[]{:S(2)}, u32[]{:S(2)}) %collective-permute-start.6) | collective-permute-done | bytes 6815776 | tf_op jit(solution)/shard_map/ppermute | solution.py:96
  1284.7 6.7 add.63
  1291.4 2.0 collective-permute-start.7
  1293.4 147.7 %collective-permute-done.7 = f32[13312,128]{0,1:T(8,128)} collective-permute-done((f32[13312,128]{0,1:T(8,128)}, f32[13312,128]{0,1:T(8,128)}, u32[]{:S(2)}, u32[]{:S(2)}) %collective-permute-start.7) | collective-permute-done | bytes 6815776 | tf_op jit(solution)/shard_map/ppermute | solution.py:96
  1441.2 5.7 add.64
  1446.9 1.0 collective-permute-start.8
  1447.9 146.2 %collective-permute-done.8 = f32[13312,128]{0,1:T(8,128)} collective-permute-done((f32[13312,128]{0,1:T(8,128)S(1)}, f32[13312,128]{0,1:T(8,128)}, u32[]{:S(2)}, u32[]{:S(2)}) %collective-permute-start.8) | collective-permute-done | bytes 6815776 | tf_op jit(solution)/shard_map/ppermute | solution.py:96
  1594.1 6.7 add.65
  1600.9 1.2 collective-permute-start.9
  1602.0 146.8 %collective-permute-done.9 = f32[13312,128]{0,1:T(8,128)} collective-permute-done((f32[13312,128]{0,1:T(8,128)}, f32[13312,128]{0,1:T(8,128)}, u32[]{:S(2)}, u32[]{:S(2)}) %collective-permute-start.9) | collective-permute-done | bytes 6815776 | tf_op jit(solution)/shard_map/ppermute | solution.py:96
  1748.8 5.7 add.66
  1754.5 5.4 fusion.31
  1760.7 3.6 all-to-all-start.9
  1765.0 5.9 all-to-all-done.9
  1772.5 11.7 cholesky.107
  1785.5 9.8 custom-call.11
  1795.6 13.1 fusion.32
  1809.5 1.7 copy.54
  (81 shorter events, 19.7 us)
Async XLA Ops:
  7.2 2.0 copy-start
  7.2 133.8 %all-gather.5.cloned.1.call-start = ((), (), s32[]{:S(2)}) async-start(), calls=%async_computation.10 | async-start | bytes 8454144 | tf_op jit(solution)/shard_map/all_gather | solution.py:35
  74.0 964.3 %all-gather.7.cloned.1.call-start = ((), (), s32[]{:S(2)}) async-start(), calls=%async_computation.11 | async-start | bytes 8454144 | tf_op jit(solution)/shard_map/all_gather | solution.py:35
  221.6 2.8 copy-start.4
  221.6 11.1 collective-permute-start
  238.5 149.0 %collective-permute-start.1 = (f32[13312,128]{0,1:T(8,128)S(1)}, f32[13312,128]{0,1:T(8,128)}, u32[]{:S(2)}, u32[]{:S(2)}) collective-permute-start(f32[13312,128]{0,1:T(8,128)S(1)} %add.55), channel_id=1, source_target_pairs={{0,8},{4,12},{8,0},{12,4},{16,24},{20,28},{24,16},{28,20},{32,40},... | collective-permute-start | bytes 20447240 | tf_op jit(solution)/shard_map/ppermute | solution.py:96
  394.1 149.8 %collective-permute-start.2 = (f32[13312,128]{0,1:T(8,128)}, f32[13312,128]{0,1:T(8,128)}, u32[]{:S(2)}, u32[]{:S(2)}) collective-permute-start(f32[13312,128]{0,1:T(8,128)} %add.56), channel_id=1, source_target_pairs={{0,16},{4,20},{8,24},{12,28},{16,0},{20,4},{24,8},{28,12},{32,48},... | collective-permute-start | bytes 20447240 | tf_op jit(solution)/shard_map/ppermute | solution.py:96
  549.7 147.2 %collective-permute-start.3 = (f32[13312,128]{0,1:T(8,128)S(1)}, f32[13312,128]{0,1:T(8,128)}, u32[]{:S(2)}, u32[]{:S(2)}) collective-permute-start(f32[13312,128]{0,1:T(8,128)S(1)} %add.57), channel_id=1, source_target_pairs={{0,32},{4,36},{8,40},{12,44},{16,48},{20,52},{24,56},{28,60},{32,0... | collective-permute-start | bytes 20447240 | tf_op jit(solution)/shard_map/ppermute | solution.py:96
  703.6 147.9 %collective-permute-start.4 = (f32[13312,128]{0,1:T(8,128)}, f32[13312,128]{0,1:T(8,128)}, u32[]{:S(2)}, u32[]{:S(2)}) collective-permute-start(f32[13312,128]{0,1:T(8,128)} %add.58), channel_id=1, source_target_pairs={{0,64},{4,68},{8,72},{12,76},{16,80},{20,84},{24,88},{28,92},{32,9... | collective-permute-start | bytes 20447240 | tf_op jit(solution)/shard_map/ppermute | solution.py:96
  857.3 5.4 copy-start.3
  1118.5 2.8 copy-start.5
  1118.5 11.5 collective-permute-start.5
  1135.7 149.0 %collective-permute-start.6 = (f32[13312,128]{0,1:T(8,128)S(1)}, f32[13312,128]{0,1:T(8,128)}, u32[]{:S(2)}, u32[]{:S(2)}) collective-permute-start(f32[13312,128]{0,1:T(8,128)S(1)} %add.62), channel_id=1, source_target_pairs={{0,8},{4,12},{8,0},{12,4},{16,24},{20,28},{24,16},{28,20},{32,40},... | collective-permute-start | bytes 20447240 | tf_op jit(solution)/shard_map/ppermute | solution.py:96
  1291.4 149.8 %collective-permute-start.7 = (f32[13312,128]{0,1:T(8,128)}, f32[13312,128]{0,1:T(8,128)}, u32[]{:S(2)}, u32[]{:S(2)}) collective-permute-start(f32[13312,128]{0,1:T(8,128)} %add.63), channel_id=1, source_target_pairs={{0,16},{4,20},{8,24},{12,28},{16,0},{20,4},{24,8},{28,12},{32,48},... | collective-permute-start | bytes 20447240 | tf_op jit(solution)/shard_map/ppermute | solution.py:96
  1446.9 147.2 %collective-permute-start.8 = (f32[13312,128]{0,1:T(8,128)S(1)}, f32[13312,128]{0,1:T(8,128)}, u32[]{:S(2)}, u32[]{:S(2)}) collective-permute-start(f32[13312,128]{0,1:T(8,128)S(1)} %add.64), channel_id=1, source_target_pairs={{0,32},{4,36},{8,40},{12,44},{16,48},{20,52},{24,56},{28,60},{32,0... | collective-permute-start | bytes 20447240 | tf_op jit(solution)/shard_map/ppermute | solution.py:96
  1600.9 147.9 %collective-permute-start.9 = (f32[13312,128]{0,1:T(8,128)}, f32[13312,128]{0,1:T(8,128)}, u32[]{:S(2)}, u32[]{:S(2)}) collective-permute-start(f32[13312,128]{0,1:T(8,128)} %add.65), channel_id=1, source_target_pairs={{0,64},{4,68},{8,72},{12,76},{16,80},{20,84},{24,88},{28,92},{32,9... | collective-permute-start | bytes 20447240 | tf_op jit(solution)/shard_map/ppermute | solution.py:96
  1754.5 5.4 copy-start.2
  1760.7 10.2 all-to-all-start.9
  1795.3 15.9 copy-start.1
Sparse Core Ops, SparseCore 0:
  74.1 66.7 all-gather.4
  971.4 66.7 all-gather.6
